TPU v7x, 32 devices: a whole 2x2x4 slice. The times are simulated.
32 devices in a mesh: tm: 8 (over z, x), height: 2 (over core), heads: 2 (over y).
Axes of the slice: x: 2, y: 2, z: 4, core: 2. Of those that a mesh axis runs over, the one named last changes fastest.
Arguments:
- queries: bfloat16 [8192, 3072], P(('tm', 'height'), 'heads'), may hold values from -50 to 50
- keys: bfloat16 [8192, 3072], P(('tm', 'height'), 'heads'), may hold values from -12 to 12
- values: bfloat16 [8192, 3072], P(('tm', 'height'), 'heads'), may hold values from -24 to 24
- residual: bfloat16 [8192, 3072], P(('tm', 'height'), 'heads'), may hold values from -3 to 3
- gate: float32 [3072], P('heads'), may hold values from -4 to 4
- out_weight: bfloat16 [3072, 3072], P('heads'), may hold values from -0.109375 to 0.109375
- far_list: int32 [16, 4], replicated, may hold values from 0 to 63, as said below
- far_count: int32 [16], replicated, may hold values from 0 to 4
Outputs:
- mixed: bfloat16 [8192, 3072], P(('tm', 'height'), 'heads')
Inputs may be any that keep to these rules, and one draw needn't show every extreme that they name: `far_list`: entries s < far_count[t] of row t name distinct blocks (tile * 4 + block within the tile) of tiles with the same row index as tile t and a frame index that differs from t's by 2 or more, at most one block of any tile; all lists that name a block of a tile u name the same block of u; entries s >= far_count[t] are 0.
All inputs are finite; a program needn't handle non-finite values.
Results may differ from a plain program's by a relative error of at most 0.011.
Values may be sent and summed in bfloat16 or wider, within the bound.
A program may use at most 256 MiB of HBM per device.

v0:
```python
import math

import jax
import jax.numpy as jnp
from jax import lax
from jax.sharding import PartitionSpec as P

HD = 128
BLOCK = 128


def with_halo(array, sides, width):
    for axis, dim in sides:
        peers, length = (lax.axis_size(axis), array.shape[dim])
        up = [(i, (i + 1) % peers) for i in range(peers - 1)]
        down = [(j, i) for i, j in up]
        last = lax.slice_in_dim(array, length - width, length, axis=dim)
        first = lax.slice_in_dim(array, 0, width, axis=dim)
        before = lax.ppermute(last, axis, up)
        after = lax.ppermute(first, axis, down)
        array = jnp.concatenate([before, array, after], axis=dim)
    return array


def local(queries, keys, values, residual, gate, out_weight, far_list, far_count):
    tile_rows, width_here = queries.shape
    heads_here = width_here // HD
    scale = 1.0 / math.sqrt(HD)
    n_frames = lax.axis_size("tm")
    n_rows = lax.axis_size("height")
    frame_pos = lax.axis_index("tm")
    row_pos = lax.axis_index("height")
    tile_here = frame_pos * n_rows + row_pos
    per_tile = tile_rows // BLOCK
    key_vals = jnp.concatenate([keys, values], axis=1)
    along_frames = with_halo(key_vals[None], (("tm", 0),), 1)
    along_rows = with_halo(key_vals[None], (("height", 0),), 1)
    prior_tile, next_tile = (along_frames[0], along_frames[2])
    below_tile, above_tile = (along_rows[0], along_rows[2])
    listed_ok = jnp.arange(far_list.shape[1])[None, :] < far_count[:, None]
    own_list = lax.dynamic_index_in_dim(far_list, tile_here, 0, False)
    own_ok = lax.dynamic_index_in_dim(listed_ok, tile_here, 0, False)
    own_source = own_list // per_tile // n_rows
    frame_ok = jnp.any(
        own_ok[None, :] & (own_source[None, :] == jnp.arange(n_frames)[:, None]), axis=1
    )
    query_heads = queries.reshape(tile_rows, heads_here, HD)

    def attend(carried, block_kv, key_ok):
        best_so_far, total, weighted = carried
        key_heads = block_kv[:, :width_here].reshape(-1, heads_here, HD)
        value_heads = block_kv[:, width_here:].reshape(-1, heads_here, HD)
        scores = (
            jnp.einsum("qhd,khd->qhk", query_heads, key_heads, preferred_element_type=jnp.float32)
            * scale
        )
        scores = jnp.where(key_ok[None, None, :], scores, jnp.float32(-1e30))
        new_best = jnp.maximum(best_so_far, jnp.max(scores, axis=-1))
        fade = jnp.exp(best_so_far - new_best)
        weights = jnp.exp(scores - new_best[..., None])
        total = total * fade + jnp.sum(weights, axis=-1)
        weighted = weighted * fade[..., None] + jnp.einsum(
            "qhk,khd->qhd",
            weights.astype(jnp.bfloat16),
            value_heads,
            preferred_element_type=jnp.float32,
        )
        return (new_best, total, weighted)

    carried = (
        jnp.full((tile_rows, heads_here), -1e30, jnp.float32),
        jnp.zeros((tile_rows, heads_here), jnp.float32),
        jnp.zeros((tile_rows, heads_here, HD), jnp.float32),
    )
    first_kv = jnp.concatenate([key_vals, prior_tile, next_tile], axis=0)
    first_ok = jnp.repeat(
        jnp.stack([frame_pos >= 0, frame_pos > 0, frame_pos < n_frames - 1]), tile_rows
    )
    carried = attend(carried, first_kv, first_ok)
    second_kv = jnp.concatenate([below_tile, above_tile], axis=0)
    second_ok = jnp.repeat(jnp.stack([row_pos > 0, row_pos < n_rows - 1]), tile_rows)
    carried = attend(carried, second_kv, second_ok)
    blocks_here = key_vals.reshape(per_tile, BLOCK, 2 * width_here)
    band_lists = lax.dynamic_index_in_dim(far_list.reshape(n_frames, n_rows, -1), row_pos, 1, False)
    band_ok = lax.dynamic_index_in_dim(listed_ok.reshape(n_frames, n_rows, -1), row_pos, 1, False)
    requested = band_ok & (band_lists // per_tile == tile_here)
    wanted = jnp.sum(jnp.where(requested, band_lists % per_tile, 0), axis=1)
    outgoing = jnp.take(blocks_here, wanted, axis=0)
    arrived = lax.all_to_all(outgoing, "tm", split_axis=0, concat_axis=0, tiled=True)
    attend_carried = carried
    slot_count = arrived.shape[0]
    group_size = math.gcd(slot_count, 16)
    for offset in range(0, slot_count, group_size):
        segment = arrived[offset : offset + group_size].reshape(group_size * BLOCK, 2 * width_here)
        segment_ok = jnp.repeat(frame_ok[offset : offset + group_size], BLOCK)
        attend_carried = attend(attend_carried, segment, segment_ok)
    carried = attend_carried
    best_so_far, total, weighted = carried
    attended = (weighted / total[..., None]).reshape(tile_rows, width_here).astype(jnp.bfloat16)
    projected = jnp.dot(attended, out_weight, preferred_element_type=jnp.float32)
    summed = lax.psum_scatter(
        projected.astype(jnp.bfloat16), "heads", scatter_dimension=1, tiled=True
    ).astype(jnp.float32)
    return (residual.astype(jnp.float32) + gate[None, :] * summed).astype(jnp.bfloat16)


def solution(mesh):
    return jax.shard_map(
        local,
        mesh=mesh,
        in_specs=(
            P(("tm", "height"), "heads"),
            P(("tm", "height"), "heads"),
            P(("tm", "height"), "heads"),
            P(("tm", "height"), "heads"),
            P("heads"),
            P("heads", None),
            P(),
            P(),
        ),
        out_specs=P(("tm", "height"), "heads"),
        check_vma=False,
    )
```

profile of v0, /device:TPU:0, one launch (start us, length us, event | category | flops | bytes accessed | tf_op | source)
XLA Modules:
  0.0 457.3 jit_solution(723632689620493707)
XLA Ops:
  12.3 3.2 fusion.47
  15.6 3.2 copy.66
  18.7 3.5 gather_fusion
  22.3 6.0 %broadcast_select_fusion = bf16[8,128,3072]{2,1,0:T(8,128)(2,1)} fusion(bf16[8,128,3072]{2,1,0:T(8,128)(2,1)} %gather_fusion, pred[8]{0:T(512)(128)(4,1)S(1)} %compare_and_fusion), kind=kLoop, calls=%fused_computation.28 | loop fusion | flops 3145728 | bytes 12582920 | tf_op jit(solution)/shard_map/jit(_take)/select_n | solution.py:88
  28.3 7.4 %all-to-all-start = ((bf16[8,128,3072]{2,1,0:T(8,128)(2,1)}), bf16[8,128,3072]{2,1,0:T(8,128)(2,1)}, u32[]{:S(2)}, u32[]{:S(2)}) async-start(bf16[8,128,3072]{2,1,0:T(8,128)(2,1)} %broadcast_select_fusion), calls=%async_computation | async-start | bytes 12582912 | tf_op jit(solution)/shard_map/all_to_all | solution.py:89
  35.7 3.1 collective-permute-start.2
  40.1 5.3 %collective-permute-start = (bf16[1,512,3072]{1,2,0:T(8,128)(2,1)}, bf16[1,512,3072]{1,2,0:T(8,128)(2,1)}, u32[]{:S(2)}, u32[]{:S(2)}) collective-permute-start(bf16[1,512,3072]{1,2,0:T(8,128)(2,1)} %get-tuple-element.16), channel_id=1, source_target_pairs={{0,4},{4,8},{8,12},{12,16},{16,20},{20,24},{24,28},{1,5},{5,9},{9,... | collective-permute-start | bytes 9437192 | tf_op jit(solution)/shard_map/ppermute | solution.py:19
  49.5 4.3 pad_maximum_fusion.1
  53.8 11.3 %bitcast_reduce_fusion.2 = (f32[512,12]{0,1:T(8,128)S(1)}, f32[12,1024,512]{2,1,0:T(8,128)}) fusion(pred[1024]{0:T(1024)(128)(4,1)S(1)} %broadcast_in_dim.89, bf16[1024,12,128]{0,2,1:T(8,128)(2,1)S(1)} %bitcast.121, bf16[512,12,128]{0,2,1:T(8,128)(2,1)S(1)} %bitcast.115), kind=kOutput, calls=%fused_computation.11 | convolution fusion | flops 1629480960 | bytes 29910016 | tf_op jit(solution)/shard_map/qhd,khd->qhk/dot_general | solution.py:54
  65.1 173.1 %collective-permute-done = bf16[1,512,3072]{1,2,0:T(8,128)(2,1)} collective-permute-done((bf16[1,512,3072]{1,2,0:T(8,128)(2,1)}, bf16[1,512,3072]{1,2,0:T(8,128)(2,1)}, u32[]{:S(2)}, u32[]{:S(2)}) %collective-permute-start) | collective-permute-done | bytes 3145760 | tf_op jit(solution)/shard_map/ppermute | solution.py:19
  238.2 16.1 %pad_maximum_fusion = bf16[1536,3072]{0,1:T(8,128)(2,1)} fusion(bf16[512,3072]{0,1:T(8,128)(2,1)} %bitcast.5, bf16[512,3072]{0,1:T(8,128)(2,1)} %bitcast.4, bf16[512,1536]{0,1:T(8,128)(2,1)S(1)} %copy-done.3, bf16[512,1536]{0,1:T(8,128)(2,1)S(1)} %copy-done.1), kind=kLoop, calls=%fused_computation.25 | loop fusion | flops 37748736 | bytes 18874368 | tf_op jit(solution)/shard_map/concatenate | solution.py:75
  254.2 7.9 %fusion.50 = (bf16[1536,1536]{0,1:T(8,128)(2,1)}, bf16[1536,1536]{0,1:T(8,128)(2,1)}) fusion(bf16[1536,3072]{0,1:T(8,128)(2,1)} %pad_maximum_fusion), kind=kLoop, calls=%fused_computation.99 | loop fusion | bytes 18874368 | tf_op jit(solution)/shard_map/slice | solution.py:52
  262.2 19.1 %bitcast_reduce_fusion = (f32[512,12]{0,1:T(8,128)S(1)}, f32[12,1536,512]{2,1,0:T(8,128)}) fusion(pred[1536]{0:T(1024)(128)(4,1)S(1)} %broadcast_in_dim.83, bf16[1536,12,128]{0,2,1:T(8,128)(2,1)} %bitcast.118, bf16[512,12,128]{0,2,1:T(8,128)(2,1)S(1)} %bitcast.116), kind=kOutput, calls=%fused_computation.2 | convolution fusion | flops 2444224512 | bytes 44066304 | tf_op jit(solution)/shard_map/qhd,khd->qhk/dot_general | solution.py:54
  281.3 5.9 %fusion.51 = (bf16[1024,1536]{1,0:T(8,128)(2,1)}, bf16[1024,1536]{1,0:T(8,128)(2,1)}) fusion(bf16[1024,3072]{1,0:T(8,128)(2,1)} %bitcast.27), kind=kLoop, calls=%fused_computation.100 | loop fusion | bytes 12582912 | tf_op jit(solution)/shard_map/slice | solution.py:51
  287.2 4.6 %copy.81 = bf16[1024,1536]{0,1:T(8,128)(2,1)} copy(bf16[1024,1536]{1,0:T(8,128)(2,1)} %get-tuple-element.14) | data formatting | bytes 6291456
  291.8 13.3 %bitcast_reduce_fusion.1 = (f32[512,12]{0,1:T(8,128)S(1)}, f32[12,1024,512]{2,1,0:T(8,128)}) fusion(pred[1024]{0:T(1024)(128)(4,1)S(1)} %broadcast_bitcast_fusion, bf16[1024,12,128]{0,2,1:T(8,128)(2,1)} %bitcast.120, bf16[512,12,128]{0,2,1:T(8,128)(2,1)S(1)} %bitcast.117), kind=kOutput, calls=%fused_computation.8 | convolution fusion | flops 1629480960 | bytes 29910016 | tf_op jit(solution)/shard_map/qhd,khd->qhk/dot_general | solution.py:54
  305.1 16.9 %fusion.1 = f32[512,12]{0,1:T(8,128)S(1)} fusion(f32[12,1536,512]{2,1,0:T(8,128)} %get-tuple-element.25, f32[512,12]{0,1:T(8,128)S(1)} %get-tuple-element.19, pred[1536]{0:T(1024)(128)(4,1)S(1)} %broadcast_in_dim.83), kind=kLoop, calls=%fused_computation.5 | loop fusion | flops 37742592 | bytes 37799424 | tf_op jit(solution)/shard_map/reduce_sum | solution.py:61
  322.1 19.3 %fusion.9 = f32[12,128,512]{2,1,0:T(8,128)} fusion(bf16[1536,12,128]{0,2,1:T(8,128)(2,1)} %bitcast.122, f32[12,1536,512]{2,1,0:T(8,128)} %get-tuple-element.25, f32[512,12]{0,1:T(8,128)S(1)} %get-tuple-element.19, pred[1536]{0:T(1024)(128)(4,1)S(1)} %broadcast_in_dim.83), kind=kOutput, calls=%fused_computation.19 | convolution fusion | flops 2453667840 | bytes 45639168 | tf_op jit(solution)/shard_map/qhk,khd->qhd/dot_general | solution.py:62
  344.2 13.5 %fusion.12 = f32[12,128,512]{2,1,0:T(8,128)} fusion(bf16[1024,12,128]{0,2,1:T(8,128)(2,1)} %bitcast.123, f32[12,1024,512]{2,1,0:T(8,128)} %get-tuple-element.21, f32[512,12]{0,1:T(8,128)S(1)} %get-tuple-element.8, pred[1024]{0:T(1024)(128)(4,1)S(1)} %broadcast_bitcast_fusion), kind=kOutput, calls=%fused_computation.21 | convolution fusion | flops 1635778560 | bytes 31482880 | tf_op jit(solution)/shard_map/qhk,khd->qhd/dot_general | solution.py:62
  357.7 19.8 %fusion.5 = (f32[512,12]{0,1:T(8,128)S(1)}, f32[512,12]{0,1:T(8,128)S(1)}) fusion(f32[12,1024,512]{2,1,0:T(8,128)} %get-tuple-element.23, f32[512,12]{0,1:T(8,128)S(1)} %get-tuple-element.9, pred[1024]{0:T(1024)(128)(4,1)S(1)} %broadcast_in_dim.89, f32[512,12]{0,1:T(8,128)S(1)} %get-tuple-element.8, f32[12,1024,512]{2,1,0:T(8,128)} %get-tuple-element.21, ...), kind=kLoop, calls=%fused_computation.15 | loop fusion | flops 50319360 | bytes 50432000 | tf_op jit(solution)/shard_map/reduce_sum | solution.py:61
  377.6 13.3 %fusion.20 = bf16[512,12,128]{0,2,1:T(8,128)(2,1)S(1)} fusion(f32[12,128,512]{2,1,0:T(8,128)} %fusion.12, f32[12,128,512]{2,1,0:T(8,128)} %fusion.9, bf16[1024,12,128]{0,2,1:T(8,128)(2,1)S(1)} %bitcast.124, f32[12,1024,512]{2,1,0:T(8,128)} %get-tuple-element.23, f32[512,12]{0,1:T(8,128)S(1)} %get-tuple-element.9, pred[1024]{0:T(1024)(128)(4,1)S(1)} %broadcast_in_dim.89, ...), kind=kOutput, calls=%fused_computation.35 | convolution fusion | flops 1641283584 | bytes 36299776 | tf_op jit(solution)/shard_map/qhk,khd->qhd/dot_general | solution.py:62
  391.0 10.3 %convolution_convert_fusion = bf16[512,3072]{1,0:T(8,128)(2,1)} fusion(bf16[512,1536]{0,1:T(8,128)(2,1)S(1)} %bitcast.126, bf16[1536,3072]{1,0:T(8,128)(2,1)} %param.13), kind=kOutput, calls=%fused_computation.29 | convolution fusion | flops 4833411072 | bytes 14155776 | tf_op jit(solution)/shard_map/dot_general | solution.py:100
  401.3 45.7 %reduce-scatter.2.cloned.1.call-done = bf16[512,1536]{1,0:T(8,128)(2,1)} async-done(((bf16[512,3072]{1,0:T(8,128)(2,1)}), bf16[512,1536]{1,0:T(8,128)(2,1)}) %reduce-scatter.2.cloned.1.call-update) | async-done | bytes 1572880 | tf_op jit(solution)/shard_map/reduce_scatter | solution.py:101
  447.0 3.0 add_convert_fusion
  (57 shorter events, 14.0 us)
Async XLA Ops:
  10.0 5.5 %copy-start = (bf16[512,1536]{0,1:T(8,128)(2,1)}, bf16[512,1536]{0,1:T(8,128)(2,1)S(1)}, u32[]{:S(2)}) copy-start(bf16[512,1536]{0,1:T(8,128)(2,1)S(1)} %copy.54) | copy-start | bytes 4718596
  12.3 3.2 copy-start.2
  28.3 18.5 %copy-start.10 = (s32[16]{0:T(128)S(1)}, s32[16]{0:T(128)}, u32[]{:S(2)}) copy-start(s32[16]{0:T(128)} %param.15) | copy-start | bytes 196
  28.3 19.1 %copy-start.6 = (bf16[512,1536]{1,0:T(8,128)(2,1)S(1)}, bf16[512,1536]{1,0:T(8,128)(2,1)}, u32[]{:S(2)}) copy-start(bf16[512,1536]{1,0:T(8,128)(2,1)} %param.8) | copy-start | bytes 4718596
  28.3 20.3 %copy-start.9 = (s32[16,4]{0,1:T(4,128)S(1)}, s32[16,4]{0,1:T(4,128)}, u32[]{:S(2)}) copy-start(s32[16,4]{0,1:T(4,128)} %param.14) | copy-start | bytes 772
  28.3 253.0 %all-to-all-start = ((bf16[8,128,3072]{2,1,0:T(8,128)(2,1)}), bf16[8,128,3072]{2,1,0:T(8,128)(2,1)}, u32[]{:S(2)}, u32[]{:S(2)}) async-start(bf16[8,128,3072]{2,1,0:T(8,128)(2,1)} %broadcast_select_fusion), calls=%async_computation | async-start | bytes 12582912 | tf_op jit(solution)/shard_map/all_to_all | solution.py:89
  35.7 411.3 %reduce-scatter.2.cloned.1.call-start = ((), (), s32[]{:S(2)}) async-start(), calls=%async_computation.2 | async-start | bytes 4718592 | tf_op jit(solution)/shard_map/reduce_scatter | solution.py:101
  35.7 13.8 %collective-permute-start.2 = (bf16[1,512,3072]{1,2,0:T(8,128)(2,1)}, bf16[1,512,3072]{1,2,0:T(8,128)(2,1)}, u32[]{:S(2)}, u32[]{:S(2)}) collective-permute-start(bf16[1,512,3072]{1,2,0:T(8,128)(2,1)} %get-tuple-element.16), channel_id=1, source_target_pairs={{0,2},{1,3},{4,6},{5,7},{8,10},{9,11},{12,14},{13,15},{16,18},{17,... | collective-permute-start | bytes 9437192 | tf_op jit(solution)/shard_map/ppermute | solution.py:19
  38.8 10.7 %collective-permute-start.3 = (bf16[1,512,3072]{1,2,0:T(8,128)(2,1)}, bf16[1,512,3072]{1,2,0:T(8,128)(2,1)}, u32[]{:S(2)}, u32[]{:S(2)}) collective-permute-start(bf16[1,512,3072]{1,2,0:T(8,128)(2,1)} %get-tuple-element.16), channel_id=1, source_target_pairs={{2,0},{3,1},{6,4},{7,5},{10,8},{11,9},{14,12},{15,13},{18,16},{19,... | collective-permute-start | bytes 9437192 | tf_op jit(solution)/shard_map/ppermute | solution.py:20
  40.1 198.0 %collective-permute-start = (bf16[1,512,3072]{1,2,0:T(8,128)(2,1)}, bf16[1,512,3072]{1,2,0:T(8,128)(2,1)}, u32[]{:S(2)}, u32[]{:S(2)}) collective-permute-start(bf16[1,512,3072]{1,2,0:T(8,128)(2,1)} %get-tuple-element.16), channel_id=1, source_target_pairs={{0,4},{4,8},{8,12},{12,16},{16,20},{20,24},{24,28},{1,5},{5,9},{9,... | collective-permute-start | bytes 9437192 | tf_op jit(solution)/shard_map/ppermute | solution.py:19
  45.5 192.7 %collective-permute-start.1 = (bf16[1,512,3072]{1,2,0:T(8,128)(2,1)}, bf16[1,512,3072]{1,2,0:T(8,128)(2,1)}, u32[]{:S(2)}, u32[]{:S(2)}) collective-permute-start(bf16[1,512,3072]{1,2,0:T(8,128)(2,1)} %get-tuple-element.16), channel_id=1, source_target_pairs={{4,0},{8,4},{12,8},{16,12},{20,16},{24,20},{28,24},{5,1},{9,5},{13... | collective-permute-start | bytes 9437192 | tf_op jit(solution)/shard_map/ppermute | solution.py:20
  53.8 184.4 %copy-start.1 = (bf16[512,1536]{0,1:T(8,128)(2,1)S(1)}, bf16[512,1536]{0,1:T(8,128)(2,1)}, u32[]{:S(2)}) copy-start(bf16[512,1536]{0,1:T(8,128)(2,1)} %copy-done) | copy-start | bytes 4718596
  53.8 184.4 %copy-start.3 = (bf16[512,1536]{0,1:T(8,128)(2,1)S(1)}, bf16[512,1536]{0,1:T(8,128)(2,1)}, u32[]{:S(2)}) copy-start(bf16[512,1536]{0,1:T(8,128)(2,1)} %copy-done.2) | copy-start | bytes 4718596
  322.1 19.3 %copy-start.4 = (bf16[1024,1536]{1,0:T(8,128)(2,1)S(1)}, bf16[1024,1536]{1,0:T(8,128)(2,1)}, u32[]{:S(2)}) copy-start(bf16[1024,1536]{1,0:T(8,128)(2,1)} %get-tuple-element.15) | copy-start | bytes 9437188
  357.7 19.8 %copy-start.5 = (bf16[1024,1536]{0,1:T(8,128)(2,1)S(1)}, bf16[1024,1536]{0,1:T(8,128)(2,1)}, u32[]{:S(2)}) copy-start(bf16[1024,1536]{0,1:T(8,128)(2,1)} %get-tuple-element.12) | copy-start | bytes 9437188
  390.9 56.1 %copy-start.7 = (bf16[512,1536]{1,0:T(8,128)(2,1)S(1)}, bf16[512,1536]{1,0:T(8,128)(2,1)}, u32[]{:S(2)}) copy-start(bf16[512,1536]{1,0:T(8,128)(2,1)} %param.11) | copy-start | bytes 4718596
  391.0 56.0 %copy-start.8 = (f32[1536]{0:T(1024)S(1)}, f32[1536]{0:T(1024)}, u32[]{:S(2)}) copy-start(f32[1536]{0:T(1024)} %param.12) | copy-start | bytes 18436
Sparse Core Ops, SparseCore 0:
  401.4 45.5 reduce-scatter.1
where the time goes:
time: 461 us; the launch traced here: 457 us
  waiting for transfers between devices  219 us (48%)
  matrix products  100 us (22%)
  other arithmetic  70.4 us (15%)
  local copies, waits for them, and re-layouts  35.5 us (8%)
  starting transfers between devices  18.5 us (4%)
  between operations  14.1 us (3%)
    ppermute x2, waiting for transfers between devices, with_halo(): before = lax.ppermute(last, axis, up)  173 us
    dot_general x3, matrix products, attend(): jnp.einsum('qhk,khd->qhd', weights.astype(jnp.bfloat16), value_heads, pre...  46.1 us
    reduce_scatter x1, waiting for transfers between devices, local(): lax.psum_scatter(projected.astype(jnp.bfloat16), 'heads', scatter_dimensi...  45.7 us
    dot_general x3, matrix products, attend(): jnp.einsum('qhd,khd->qhk', query_heads, key_heads, preferred_element_type...  43.6 us
    reduce_sum x2, other arithmetic, attend(): total = total * fade + jnp.sum(weights, axis=-1)  36.7 us
    concatenate x1, other arithmetic, local(): first_kv = jnp.concatenate([key_vals, prior_tile, next_tile], axis=0)  16.1 us
    unnamed x28, local copies, waits for them, and re-layouts  13.2 us
    dot_general x1, matrix products, local(): jnp.dot(attended, out_weight, preferred_element_type=jnp.float32)  10.3 us
  transfers between devices with their start and end apart: 6, of which 2 were waited for; matrix products, arithmetic and copies ran while one was open for 13% of the time, Pallas kernels for 0%

commit v1 on v0

--- a/solution.py
+++ b/solution.py
@@ -1,12 +1,18 @@
+import functools
 import math
 
 import jax
 import jax.numpy as jnp
 from jax import lax
+from jax.experimental import pallas as pl
+from jax.experimental.pallas import tpu as pltpu
 from jax.sharding import PartitionSpec as P
 
 HD = 128
 BLOCK = 128
+GROUPS = 3
+Q_ROWS = 256
+EXP2_SCALE = math.log2(math.e) / math.sqrt(HD)
 
 
 def with_halo(array, sides, width):
@@ -22,7 +28,7 @@
     return array
 
 
-def local(queries, keys, values, residual, gate, out_weight, far_list, far_count):
+def plain_local(queries, keys, values, residual, gate, out_weight, far_list, far_count):
     tile_rows, width_here = queries.shape
     heads_here = width_here // HD
     scale = 1.0 / math.sqrt(HD)
@@ -104,7 +110,168 @@
     return (residual.astype(jnp.float32) + gate[None, :] * summed).astype(jnp.bfloat16)
 
 
+def attention_kernel(far_entries, info, mine, got, side_mine, side_got, near_mine, near_got, far, out):
+    f32 = jnp.float32
+    rows = mine.shape[1]
+    ones = jnp.ones((rows, HD), jnp.bfloat16)
+    far_rows = far_entries * BLOCK
+    for p in range(2):
+        own, other = ((mine, got), (got, mine))[p]
+        side = (side_mine, side_got)[p]
+        near = (near_mine, near_got)[p]
+        picked = [(info[p, 2 * s], info[p, 2 * s + 1]) for s in range(far_entries)]
+        far_k = jnp.concatenate([far[z, j, 0] for z, j in picked], axis=0)
+        far_v = jnp.concatenate([far[z, j, 1] for z, j in picked], axis=0)
+        count = info[p, 2 * far_entries]
+        near_ok = info[p, 2 * far_entries + 1]
+        block_of = lax.broadcasted_iota(jnp.int32, (1, far_rows), 1) // BLOCK
+        far_bias = jnp.where(block_of < count, f32(0), f32(-1e30))
+        near_bias = jnp.where(
+            jnp.full((1, rows), near_ok, jnp.int32) > 0, f32(0), f32(-1e30)
+        )
+        pieces = [
+            (own[0], own[1], None),
+            (other[0], other[1], None),
+            (side[0], side[1], None),
+            (near[0], near[1], near_bias),
+            (far_k, far_v, far_bias),
+        ]
+        for q0 in range(0, rows, Q_ROWS):
+            q = own[2, q0 : q0 + Q_ROWS]
+            scores = []
+            for k, _, bias in pieces:
+                s = lax.dot_general(q, k, (((1,), (1,)), ((), ())), preferred_element_type=f32)
+                scores.append(s if bias is None else s + bias)
+            largest = scores[0].max(axis=1, keepdims=True)
+            for s in scores[1:]:
+                largest = jnp.maximum(largest, s.max(axis=1, keepdims=True))
+            total = jnp.zeros((Q_ROWS, 2 * HD), f32)
+            for s, (_, v, _) in zip(scores, pieces):
+                weights = jnp.exp2((s - largest) * EXP2_SCALE).astype(jnp.bfloat16)
+                v_ones = jnp.concatenate([v, ones[: v.shape[0]]], axis=1)
+                total = total + jnp.dot(weights, v_ones, preferred_element_type=f32)
+            out[p, q0 : q0 + Q_ROWS] = (total[:, :HD] / total[:, HD:]).astype(jnp.bfloat16)
+
+
+def attention(info, mine, got, side_mine, side_got, near_mine, near_got, far):
+    rows, width = mine.shape[1:]
+    far_entries = (info.shape[1] - 2) // 2
+
+    def spec(array):
+        lead = array.shape[:-1]
+        return pl.BlockSpec(lead + (HD,), lambda h: (0,) * len(lead) + (h,))
+
+    arrays = (mine, got, side_mine, side_got, near_mine, near_got, far)
+    keys = 4 * rows + far_entries * BLOCK
+    return pl.pallas_call(
+        functools.partial(attention_kernel, far_entries),
+        grid=(width // HD,),
+        out_shape=jax.ShapeDtypeStruct((2, rows, width), jnp.bfloat16),
+        in_specs=[pl.BlockSpec(memory_space=pltpu.SMEM)] + [spec(a) for a in arrays],
+        out_specs=pl.BlockSpec((2, rows, HD), lambda h: (0, 0, h)),
+        compiler_params=pltpu.CompilerParams(vmem_limit_bytes=48 * 2**20),
+        cost_estimate=pl.CostEstimate(
+            flops=2 * rows * keys * width * 8,
+            bytes_accessed=sum(a.size * 2 for a in arrays),
+            transcendentals=2 * rows * keys * width // HD,
+        ),
+    )(info, *arrays)
+
+
+def paired_local(queries, keys, values, residual, gate, out_weight, far_list, far_count):
+    rows, width = queries.shape
+    half = width // 2
+    n_frames, n_rows = lax.axis_size("tm"), lax.axis_size("height")
+    frame, row = lax.axis_index("tm"), lax.axis_index("height")
+    group_y = lax.axis_index("heads")
+    x, z = frame % 2, frame // 2
+    n_z = n_frames // 2
+    per_tile = rows // BLOCK
+    far_entries = far_list.shape[1]
+    swap_x = [(i, i ^ 1) for i in range(n_frames)]
+    direct = [(2 * i + 1, 2 * i + 3) for i in range(n_z - 1)]
+    direct += [(2 * i + 2, 2 * i) for i in range(n_z - 1)]
+    onward = [(2 * i, 2 * i + 2) for i in range(n_z - 1)]
+    onward += [(2 * i + 3, 2 * i + 1) for i in range(n_z - 1)]
+    swap = [(0, 1), (1, 0)]
+
+    listed_ok = jnp.arange(far_entries)[None, :] < far_count[:, None]
+    tiles = jnp.arange(n_frames * n_rows)
+    named = listed_ok[None] & (far_list[None] // per_tile == tiles[:, None, None])
+    offered = jnp.max(jnp.where(named, far_list[None] % per_tile, 0), axis=(1, 2))
+    info_rows = []
+    for p, f in ((0, frame), (1, frame ^ 1)):
+        t = f * n_rows + row
+        source = far_list[t] // per_tile // n_rows
+        pairs = jnp.stack([source // 2, (source % 2) ^ x], axis=1).reshape(-1)
+        parity = x ^ p
+        near_ok = jnp.where(parity == 0, z > 0, z < n_z - 1).astype(jnp.int32)
+        info_rows.append(jnp.concatenate([pairs, jnp.stack([far_count[t], near_ok])]))
+    info = jnp.stack(info_rows).astype(jnp.int32)
+    off_mine = offered[frame * n_rows + row] * BLOCK
+    off_got = offered[(frame ^ 1) * n_rows + row] * BLOCK
+
+    wide = width // n_rows
+    w_theirs = lax.dynamic_slice(out_weight, (row * wide, (1 - group_y) * width), (wide, width))
+    w_first = lax.ppermute(w_theirs, "heads", swap)
+    w_second = lax.ppermute(w_first, "height", swap)
+    w_other = jnp.where(
+        row == 0,
+        jnp.concatenate([w_first, w_second], axis=0),
+        jnp.concatenate([w_second, w_first], axis=0),
+    )
+    w_own = lax.dynamic_slice(out_weight, (0, group_y * width), (width, width))
+
+    step = half // GROUPS
+    projected = None
+    for g in range(GROUPS):
+        here = x * half + g * step
+        there = (1 - x) * half + g * step
+
+        def cut(array, start):
+            return lax.dynamic_slice(array, (0, start), (rows, step))
+
+        got_kv = lax.ppermute(jnp.stack([cut(keys, there), cut(values, there)]), "tm", swap_x)
+        got_q = lax.ppermute(cut(queries, there), "tm", swap_x)
+        mine_kv = jnp.stack([cut(keys, here), cut(values, here)])
+        mine = jnp.concatenate([mine_kv, cut(queries, here)[None]])
+        got = jnp.concatenate([got_kv, got_q[None]])
+        near_got = lax.ppermute(mine_kv, "tm", direct)
+        near_mine = lax.ppermute(got_kv, "tm", onward)
+        side_mine = lax.ppermute(mine_kv, "height", swap)
+        side_got = lax.ppermute(got_kv, "height", swap)
+        offer = jnp.stack([
+            lax.dynamic_slice(mine_kv, (0, off_mine, 0), (2, BLOCK, step)),
+            lax.dynamic_slice(got_kv, (0, off_got, 0), (2, BLOCK, step)),
+        ])
+        far = lax.all_gather(
+            offer, "tm",
+            axis_index_groups=[[2 * i + e for i in range(n_z)] for e in range(2)],
+        )
+        done = attention(info, mine, got, side_mine, side_got, near_mine, near_got, far)
+        back = lax.ppermute(done[1], "tm", swap_x)
+        both = jnp.concatenate([done[0], back], axis=1)
+        across = lax.ppermute(both, "heads", swap)
+        w_rows = [
+            lax.dynamic_slice(w, (s, 0), (step, width))
+            for w in (w_own, w_other) for s in (here, there)
+        ]
+        part = jnp.dot(both, jnp.concatenate(w_rows[:2]), preferred_element_type=jnp.float32)
+        part = part + jnp.dot(across, jnp.concatenate(w_rows[2:]), preferred_element_type=jnp.float32)
+        projected = part if projected is None else projected + part
+    return (residual.astype(jnp.float32) + gate[None, :] * projected).astype(jnp.bfloat16)
+
+
 def solution(mesh):
+    sizes = dict(mesh.shape)
+
+    def local(queries, *rest):
+        width = queries.shape[1]
+        paired = sizes["tm"] % 2 == 0 and sizes["height"] == 2 and sizes["heads"] == 2
+        if paired and width % (2 * GROUPS * HD) == 0:
+            return paired_local(queries, *rest)
+        return plain_local(queries, *rest)
+
     return jax.shard_map(
         local,
         mesh=mesh,

time: 461 us -> 206 us (0.45)
  waiting for transfers between devices: 219 us -> 60.5 us
  matrix products: 100 us -> 10.3 us
  other arithmetic: 70.4 us -> 21.8 us
  Pallas kernels: 0 us -> 27 us
  starting transfers between devices: 18.5 us -> 41.5 us
  local copies, waits for them, and re-layouts: 35.5 us -> 29.1 us
    ppermute x4 -> x26, waiting for transfers between devices: 173 us -> 60.4 us  [the longest x3 22 us: paired_local(): lax.ppermute(jnp.stack([cut(keys, there), cut(values, there)]), 'tm', swa...]
    dot_general x7 -> x6, matrix products: 100 us -> 10.3 us  [the longest x3 7.32 us: paired_local(): jnp.dot(both, jnp.concatenate(w_rows[:2]), preferred_element_type=jnp.flo...]
    reduce_scatter x1 -> x0, waiting for transfers between devices: 45.7 us -> none  [local(): lax.psum_scatter(projected.astype(jnp.bfloat16), 'heads', scatter_dimensi...]
    reduce_sum x3 -> x0, other arithmetic: 36.8 us -> none  [the longest x2 36.7 us: attend(): total = total * fade + jnp.sum(weights, axis=-1)]
    ppermute x4 -> x26, starting transfers between devices: 11 us -> 41.4 us  [the longest x3 17 us: paired_local(): near_mine = lax.ppermute(got_kv, 'tm', onward)]
    pallas_call x0 -> x3, Pallas kernels: none -> 27 us  [attention(): pl.pallas_call(functools.partial(attention_kernel, far_entries), grid=(wi...]
    slice x2 -> x0, local copies, waits for them, and re-layouts: 13.9 us -> none  [the longest x1 7.94 us: attend(): value_heads = block_kv[:, width_here:].reshape(-1, heads_here, HD)]
    dynamic_slice x4 -> x6, local copies, waits for them, and re-layouts: 0.68 us -> 13.8 us  [the longest x2 7.36 us: paired_local(): lax.dynamic_slice(w, (s, 0), (step, width))]
  transfers between devices with their start and end apart: 6 -> 29, of which waited for: 2 -> 9; matrix products, arithmetic and copies ran while one was open for 13% -> 22% of each run, Pallas kernels for 0% -> 13%
where the time goes in v1:
time: 206 us; the launch traced here: 205 us
  waiting for transfers between devices  60.5 us (29%)
  starting transfers between devices  41.5 us (20%)
  local copies, waits for them, and re-layouts  29.1 us (14%)
  Pallas kernels  27 us (13%)
  other arithmetic  21.8 us (11%)
  between operations  14.8 us (7%)
  matrix products  10.3 us (5%)
    pallas_call x3, Pallas kernels, attention(): pl.pallas_call(functools.partial(attention_kernel, far_entries), grid=(wi...  27 us
    ppermute x3, waiting for transfers between devices, paired_local(): lax.ppermute(jnp.stack([cut(keys, there), cut(values, there)]), 'tm', swa...  22 us
    ppermute x3, waiting for transfers between devices, paired_local(): across = lax.ppermute(both, 'heads', swap)  18.4 us
    ppermute x3, starting transfers between devices, paired_local(): near_mine = lax.ppermute(got_kv, 'tm', onward)  17 us
    ppermute x3, waiting for transfers between devices, paired_local(): near_mine = lax.ppermute(got_kv, 'tm', onward)  11.7 us
    unnamed x36, local copies, waits for them, and re-layouts  8.59 us
    ppermute x3, waiting for transfers between devices, paired_local(): got_q = lax.ppermute(cut(queries, there), 'tm', swap_x)  8.33 us
    dynamic_slice x2, local copies, waits for them, and re-layouts, paired_local(): lax.dynamic_slice(w, (s, 0), (step, width))  7.36 us
  transfers between devices with their start and end apart: 29, of which 9 were waited for; matrix products, arithmetic and copies ran while one was open for 22% of the time, Pallas kernels for 13%

profile of v1, /device:TPU:0, one launch (start us, length us, event | category | flops | bytes accessed | tf_op | source)
XLA Modules:
  0.0 205.0 jit_solution(5266709848664187836)
XLA Ops:
  6.5 2.1 %dynamic-slice_bitcast_fusion.10 = (bf16[1,512,256]{2,1,0:T(8,128)(2,1)S(1)}, bf16[1,512,256]{2,1,0:T(8,128)(2,1)S(1)}, bf16[1,512,256]{2,1,0:T(8,128)(2,1)S(1)}...) fusion(bf16[512,1536]{1,0:T(8,128)(2,1)} %param.10, ...), kind=kLoop, calls=%fused_computation.70 | loop fusion | bytes 6291480 | tf_op jit(solution)/shard_map/stack | solution.py:234
  8.7 3.0 %collective-permute-start.18 = (bf16[2,512,256]{2,1,0:T(8,128)(2,1)S(1)}, bf16[2,512,256]{2,1,0:T(8,128)(2,1)}, u32[]{:S(2)}, u32[]{:S(2)}) collective-permute-start(bf16[2,512,256]{2,1,0:T(8,128)(2,1)S(1)} %pad_maximum_fusion.13), channel_id=1, source_target_pairs={{0,4},{4,0},{8,12},{12,8},{16,20},{20,16},{24,28},{28,24},{1,5},{5... | collective-permute-start | bytes 1572872 | tf_op jit(solution)/shard_map/ppermute | solution.py:234
  13.8 10.0 %collective-permute-done.18 = bf16[2,512,256]{2,1,0:T(8,128)(2,1)} collective-permute-done((bf16[2,512,256]{2,1,0:T(8,128)(2,1)S(1)}, bf16[2,512,256]{2,1,0:T(8,128)(2,1)}, u32[]{:S(2)}, u32[]{:S(2)}) %collective-permute-start.18) | collective-permute-done | bytes 524320 | tf_op jit(solution)/shard_map/ppermute | solution.py:234
  28.0 2.3 %constant_dynamic-slice_fusion.8 = (bf16[512,256]{1,0:T(8,128)(2,1)}, bf16[512,256]{1,0:T(8,128)(2,1)}, bf16[1,512,256]{2,1,0:T(8,128)(2,1)S(1)}, bf16[1,512,256...) fusion(bf16[512,1536]{1,0:T(8,128)(2,1)} %param.8, s32[]{:T(128)S(6)} %select_n.245, ...), kind=kLoop, calls=%fused_computation.95 | loop fusion | bytes 3145752 | tf_op jit(solution)/shard_map/dynamic_slice | solution.py:232
  30.7 3.3 %dynamic_slice.146 = bf16[768,1536]{1,0:T(8,128)(2,1)} dynamic-slice(bf16[1536,3072]{1,0:T(8,128)(2,1)} %param.13, s32[]{:T(128)S(6)} %select_n.256, s32[]{:T(128)S(6)} %select_n.257), dynamic_slice_sizes={768,1536} | dynamic-slice | bytes 4718596 | tf_op jit(solution)/shard_map/dynamic_slice | solution.py:215
  38.8 2.5 %collective-permute-done.10 = bf16[2,512,256]{2,1,0:T(8,128)(2,1)S(1)} collective-permute-done((bf16[2,512,256]{2,1,0:T(8,128)(2,1)}, bf16[2,512,256]{2,1,0:T(8,128)(2,1)S(1)}, u32[]{:S(2)}, u32[]{:S(2)}) %collective-permute-start.10) | collective-permute-done | bytes 524320 | tf_op jit(solution)/shard_map/ppermute | solution.py:234
  48.7 4.0 %collective-permute-done.11 = bf16[512,256]{1,0:T(8,128)(2,1)} collective-permute-done((bf16[512,256]{1,0:T(8,128)(2,1)}, bf16[512,256]{1,0:T(8,128)(2,1)}, u32[]{:S(2)}, u32[]{:S(2)}) %collective-permute-start.11) | collective-permute-done | bytes 262176 | tf_op jit(solution)/shard_map/ppermute | solution.py:235
  54.0 4.3 %collective-permute-done.1 = bf16[512,256]{1,0:T(8,128)(2,1)} collective-permute-done((bf16[512,256]{1,0:T(8,128)(2,1)}, bf16[512,256]{1,0:T(8,128)(2,1)}, u32[]{:S(2)}, u32[]{:S(2)}) %collective-permute-start.1) | collective-permute-done | bytes 262176 | tf_op jit(solution)/shard_map/ppermute | solution.py:235
  58.3 9.5 %collective-permute-done = bf16[2,512,256]{2,1,0:T(8,128)(2,1)} collective-permute-done((bf16[2,512,256]{2,1,0:T(8,128)(2,1)}, bf16[2,512,256]{2,1,0:T(8,128)(2,1)}, u32[]{:S(2)}, u32[]{:S(2)}) %collective-permute-start) | collective-permute-done | bytes 524320 | tf_op jit(solution)/shard_map/ppermute | solution.py:234
  67.8 4.2 %collective-permute-start.22 = (bf16[2,512,256]{2,1,0:T(8,128)(2,1)}, bf16[2,512,256]{2,1,0:T(8,128)(2,1)}, u32[]{:S(2)}, u32[]{:S(2)}) collective-permute-start(bf16[2,512,256]{2,1,0:T(8,128)(2,1)} %collective-permute-done.18), channel_id=1, source_target_pairs={{0,8},{8,16},{16,24},{12,4},{20,12},{28,20},{1,9},{9,17},{17,25},{... | collective-permute-start | bytes 1572872 | tf_op jit(solution)/shard_map/ppermute | solution.py:240
  75.8 2.2 %pad_maximum_fusion.3.got = bf16[3,512,256]{2,1,0:T(8,128)(2,1)} fusion(bf16[1,512,256]{2,1,0:T(8,128)(2,1)} %bitcast.22, bf16[2,512,256]{2,1,0:T(8,128)(2,1)} %copy-done.14), kind=kLoop, calls=%fused_computation.33 | loop fusion | flops 393216 | bytes 1572864 | tf_op jit(solution)/shard_map/concatenate | solution.py:238
  80.6 11.7 %collective-permute-done.22.near_mine = bf16[2,512,256]{2,1,0:T(8,128)(2,1)} collective-permute-done((bf16[2,512,256]{2,1,0:T(8,128)(2,1)}, bf16[2,512,256]{2,1,0:T(8,128)(2,1)}, u32[]{:S(2)}, u32[]{:S(2)}) %collective-permute-start.22) | collective-permute-done | bytes 524320 | tf_op jit(solution)/shard_map/ppermute | solution.py:240
  92.3 5.2 %collective-permute-start.14 = (bf16[2,512,256]{2,1,0:T(8,128)(2,1)}, bf16[2,512,256]{2,1,0:T(8,128)(2,1)}, u32[]{:S(2)}, u32[]{:S(2)}) collective-permute-start(bf16[2,512,256]{2,1,0:T(8,128)(2,1)} %copy-done.14), channel_id=1, source_target_pairs={{0,8},{8,16},{16,24},{12,4},{20,12},{28,20},{1,9},{9,17},{17,25},{... | collective-permute-start | bytes 1572872 | tf_op jit(solution)/shard_map/ppermute | solution.py:240
  102.1 8.9 %shard_map.84 = bf16[2,512,256]{2,1,0:T(8,128)(2,1)S(1)} custom-call(s32[2,10]{1,0:T(2,128)S(1)} %pad_add_fusion.2.info, bf16[3,512,256]{2,1,0:T(8,128)(2,1)S(1)} %pad_maximum_fusion.4.mine, bf16[3,512,256]{2,1,0:T(8,128)(2,1)S(1)} %copy-done.1, bf16[2,512,256]{2,1,0:T(8,128)(2,1)S(1)} %copy-done.8, bf16[2,512,256]{2,1,0:T(8,128)(2,1)} %collective-permute-done.21.side_got, ...), custom_call_target="tpu_custom_call" | custom-call | flops 5368709120 | bytes 4718592 | tf_op jit(solution)/shard_map/pallas_call | solution.py:166
  113.7 7.6 %collective-permute-start.4 = (bf16[2,512,256]{2,1,0:T(8,128)(2,1)}, bf16[2,512,256]{2,1,0:T(8,128)(2,1)}, u32[]{:S(2)}, u32[]{:S(2)}) collective-permute-start(bf16[2,512,256]{2,1,0:T(8,128)(2,1)} %collective-permute-done), channel_id=1, source_target_pairs={{0,8},{8,16},{16,24},{12,4},{20,12},{28,20},{1,9},{9,17},{17,25},{... | collective-permute-start | bytes 1572872 | tf_op jit(solution)/shard_map/ppermute | solution.py:240
  123.7 9.0 %shard_map.83 = bf16[2,512,256]{2,1,0:T(8,128)(2,1)S(1)} custom-call(s32[2,10]{1,0:T(2,128)S(1)} %pad_add_fusion.2.info, bf16[3,512,256]{2,1,0:T(8,128)(2,1)S(1)} %pad_maximum_fusion.2.mine, bf16[3,512,256]{2,1,0:T(8,128)(2,1)S(1)} %copy-done, bf16[2,512,256]{2,1,0:T(8,128)(2,1)} %collective-permute-done.12.side_mine, ...), custom_call_target="tpu_custom_call" | custom-call | flops 5368709120 | bytes 4718592 | tf_op jit(solution)/shard_map/pallas_call | solution.py:166
  137.6 9.1 %shard_map.82 = bf16[2,512,256]{2,1,0:T(8,128)(2,1)S(1)} custom-call(s32[2,10]{1,0:T(2,128)S(1)} %pad_add_fusion.2.info, bf16[3,512,256]{2,1,0:T(8,128)(2,1)S(1)} %pad_maximum_fusion.mine, bf16[3,512,256]{2,1,0:T(8,128)(2,1)S(1)} %pad_maximum_fusion.1.got, bf16[2,512,256]{2,1,0:T(8,128)(2,1)} %collective-permute-done.2.side_mine, ...), custom_call_target="tpu_custom_call" | custom-call | flops 5368709120 | bytes 4718592 | tf_op jit(solution)/shard_map/pallas_call | solution.py:166
  147.5 3.2 %collective-permute-start.6 = (bf16[512,256]{1,0:T(8,128)(2,1)}, bf16[512,256]{1,0:T(8,128)(2,1)}, u32[]{:S(2)}, u32[]{:S(2)}) collective-permute-start(bf16[512,256]{1,0:T(8,128)(2,1)} %get-tuple-element.38), channel_id=1, source_target_pairs={{0,4},{4,0},{8,12},{12,8},{16,20},{20,16},{24,28},{28,24},{1,5},{5... | collective-permute-start | bytes 786440 | tf_op jit(solution)/shard_map/ppermute | solution.py:252
  150.7 7.0 %fusion.44 = (bf16[256,1536]{1,0:T(8,128)(2,1)S(1)}, bf16[256,1536]{1,0:T(8,128)(2,1)S(1)}, bf16[256,1536]{1,0:T(8,128)(2,1)S(1)}, bf16[256,1536]{1,0:T(8,128)(2...) fusion(bf16[1536,3072]{1,0:T(8,128)(2,1)} %param.13, s32[]{:T(128)S(6)} %select_n.251, s32[]{:T(128)S(6)} %select_n.253, ...), kind=kLoop, calls=%fused_computation.150 | loop fusion | bytes 9437212 | tf_op jit(solution)/shard_map/dynamic_slice | solution.py:256
  164.5 4.9 %maximum_select_fusion = bf16[1536,1536]{1,0:T(8,128)(2,1)S(1)} fusion(bf16[768,1536]{1,0:T(8,128)(2,1)} %collective-permute-done.9, bf16[768,1536]{1,0:T(8,128)(2,1)} %collective-permute-done.8, pred[]{:T(512)S(6)} %eq.34), kind=kLoop, calls=%fused_computation | loop fusion | flops 21233664 | bytes 9437185 | tf_op jit(solution)/shard_map/jit(_where)/select_n | solution.py:218
  169.7 4.1 %collective-permute-done.25 = bf16[512,512]{1,0:T(8,128)(2,1)S(1)} collective-permute-done((bf16[512,512]{1,0:T(8,128)(2,1)S(1)}, bf16[512,512]{1,0:T(8,128)(2,1)S(1)}, u32[]{:S(2)}, u32[]{:S(2)}) %collective-permute-start.25) | collective-permute-done | bytes 524320 | tf_op jit(solution)/shard_map/ppermute | solution.py:254
  176.7 8.3 %collective-permute-done.17 = bf16[512,512]{1,0:T(8,128)(2,1)S(1)} collective-permute-done((bf16[512,512]{1,0:T(8,128)(2,1)S(1)}, bf16[512,512]{1,0:T(8,128)(2,1)S(1)}, u32[]{:S(2)}, u32[]{:S(2)}) %collective-permute-start.17) | collective-permute-done | bytes 524320 | tf_op jit(solution)/shard_map/ppermute | solution.py:254
  188.0 6.1 %collective-permute-done.7 = bf16[512,512]{1,0:T(8,128)(2,1)S(1)} collective-permute-done((bf16[512,512]{1,0:T(8,128)(2,1)S(1)}, bf16[512,512]{1,0:T(8,128)(2,1)S(1)}, u32[]{:S(2)}, u32[]{:S(2)}) %collective-permute-start.7) | collective-permute-done | bytes 524320 | tf_op jit(solution)/shard_map/ppermute | solution.py:254
  195.0 3.4 %fusion.4 = bf16[512,1536]{1,0:T(8,128)(2,1)} fusion(f32[512,1536]{1,0:T(8,128)S(1)} %convolution_add_fusion, f32[512,1536]{1,0:T(8,128)S(1)} %convolution_add_fusion.1, f32[512,1536]{1,0:T(8,128)S(1)} %fusion.8, bf16[512,1536]{1,0:T(8,128)(2,1)S(1)} %copy-done.13, bf16[256,1536]{1,0:T(8,128)(2,1)S(1)} %get-tuple-element.10, ...), kind=kOutput, calls=%fused_computation.8 | convolution fusion | flops 815005696 | bytes 14686208 | tf_op jit(solution)/shard_map/dot_general | solution.py:259
  (130 shorter events, 54.4 us)
Async XLA Ops:
  6.5 92.2 %all-gather.11.cloned.1.call-start = ((), (), s32[]{:S(2)}) async-start(), calls=%async_computation.2 | async-start | bytes 1310720 | tf_op jit(solution)/shard_map/all_gather | solution.py:247
  25.4 95.9 %all-gather.9.cloned.1.call-start = ((), (), s32[]{:S(2)}) async-start(), calls=%async_computation.1 | async-start | bytes 1310720 | tf_op jit(solution)/shard_map/all_gather | solution.py:247
  30.4 18.3 %collective-permute-start.19 = (bf16[512,256]{1,0:T(8,128)(2,1)}, bf16[512,256]{1,0:T(8,128)(2,1)}, u32[]{:S(2)}, u32[]{:S(2)}) collective-permute-start(bf16[512,256]{1,0:T(8,128)(2,1)} %get-tuple-element.35), channel_id=1, source_target_pairs={{0,4},{4,0},{8,12},{12,8},{16,20},{20,16},{24,28},{28,24},{1,5},{5... | collective-permute-start | bytes 786440 | tf_op jit(solution)/shard_map/ppermute | solution.py:235
  33.9 87.4 %collective-permute-start.8 = (bf16[768,1536]{1,0:T(8,128)(2,1)}, bf16[768,1536]{1,0:T(8,128)(2,1)}, u32[]{:S(2)}, u32[]{:S(2)}) collective-permute-start(bf16[768,1536]{1,0:T(8,128)(2,1)} %dynamic_slice.146), channel_id=1, source_target_pairs={{0,1},{1,0},{2,3},{3,2},{4,5},{5,4},{6,7},{7,6},{8,9},{9,8},{10,11... | collective-permute-start | bytes 7077896 | tf_op jit(solution)/shard_map/ppermute | solution.py:216
  37.2 21.1 %collective-permute-start.1 = (bf16[512,256]{1,0:T(8,128)(2,1)}, bf16[512,256]{1,0:T(8,128)(2,1)}, u32[]{:S(2)}, u32[]{:S(2)}) collective-permute-start(bf16[512,256]{1,0:T(8,128)(2,1)} %get-tuple-element.31), channel_id=1, source_target_pairs={{0,4},{4,0},{8,12},{12,8},{16,20},{20,16},{24,28},{28,24},{1,5},{5... | collective-permute-start | bytes 786440 | tf_op jit(solution)/shard_map/ppermute | solution.py:235
  41.4 26.4 %collective-permute-start = (bf16[2,512,256]{2,1,0:T(8,128)(2,1)}, bf16[2,512,256]{2,1,0:T(8,128)(2,1)}, u32[]{:S(2)}, u32[]{:S(2)}) collective-permute-start(bf16[2,512,256]{2,1,0:T(8,128)(2,1)} %pad_maximum_fusion.9), channel_id=1, source_target_pairs={{0,4},{4,0},{8,12},{12,8},{16,20},{20,16},{24,28},{28,24},{1,5},{5... | collective-permute-start | bytes 1572872 | tf_op jit(solution)/shard_map/ppermute | solution.py:234
  43.9 92.6 %all-gather.7.cloned.1.call-start = ((), (), s32[]{:S(2)}) async-start(), calls=%async_computation | async-start | bytes 1310720 | tf_op jit(solution)/shard_map/all_gather | solution.py:247
  48.6 29.3 %collective-permute-start.20 = (bf16[2,512,256]{2,1,0:T(8,128)(2,1)}, bf16[2,512,256]{2,1,0:T(8,128)(2,1)S(1)}, u32[]{:S(2)}, u32[]{:S(2)}) collective-permute-start(bf16[2,512,256]{2,1,0:T(8,128)(2,1)} %pad_maximum_fusion.8), channel_id=1, source_target_pairs={{0,2},{2,0},{1,3},{3,1},{4,6},{6,4},{5,7},{7,5},{8,10},{10,8},{9,1... | collective-permute-start | bytes 1572872 | tf_op jit(solution)/shard_map/ppermute | solution.py:241
  52.7 26.0 %collective-permute-start.23 = (bf16[2,512,256]{2,1,0:T(8,128)(2,1)}, bf16[2,512,256]{2,1,0:T(8,128)(2,1)}, u32[]{:S(2)}, u32[]{:S(2)}) collective-permute-start(bf16[2,512,256]{2,1,0:T(8,128)(2,1)} %pad_maximum_fusion.8), channel_id=1, source_target_pairs={{4,12},{12,20},{20,28},{8,0},{16,8},{24,16},{5,13},{13,21},{21,29}... | collective-permute-start | bytes 1572872 | tf_op jit(solution)/shard_map/ppermute | solution.py:239
  58.3 21.7 %collective-permute-start.21 = (bf16[2,512,256]{2,1,0:T(8,128)(2,1)}, bf16[2,512,256]{2,1,0:T(8,128)(2,1)}, u32[]{:S(2)}, u32[]{:S(2)}) collective-permute-start(bf16[2,512,256]{2,1,0:T(8,128)(2,1)} %collective-permute-done.18), channel_id=1, source_target_pairs={{0,2},{2,0},{1,3},{3,1},{4,6},{6,4},{5,7},{7,5},{8,10},{10,8},{9,1... | collective-permute-start | bytes 1572872 | tf_op jit(solution)/shard_map/ppermute | solution.py:242
  67.8 24.5 %collective-permute-start.22 = (bf16[2,512,256]{2,1,0:T(8,128)(2,1)}, bf16[2,512,256]{2,1,0:T(8,128)(2,1)}, u32[]{:S(2)}, u32[]{:S(2)}) collective-permute-start(bf16[2,512,256]{2,1,0:T(8,128)(2,1)} %collective-permute-done.18), channel_id=1, source_target_pairs={{0,8},{8,16},{16,24},{12,4},{20,12},{28,20},{1,9},{9,17},{17,25},{... | collective-permute-start | bytes 1572872 | tf_op jit(solution)/shard_map/ppermute | solution.py:240
  78.7 33.1 %collective-permute-start.12 = (bf16[2,512,256]{2,1,0:T(8,128)(2,1)}, bf16[2,512,256]{2,1,0:T(8,128)(2,1)}, u32[]{:S(2)}, u32[]{:S(2)}) collective-permute-start(bf16[2,512,256]{2,1,0:T(8,128)(2,1)} %pad_maximum_fusion.7), channel_id=1, source_target_pairs={{0,2},{2,0},{1,3},{3,1},{4,6},{6,4},{5,7},{7,5},{8,10},{10,8},{9,1... | collective-permute-start | bytes 1572872 | tf_op jit(solution)/shard_map/ppermute | solution.py:241
  78.7 33.1 %collective-permute-start.15 = (bf16[2,512,256]{2,1,0:T(8,128)(2,1)}, bf16[2,512,256]{2,1,0:T(8,128)(2,1)}, u32[]{:S(2)}, u32[]{:S(2)}) collective-permute-start(bf16[2,512,256]{2,1,0:T(8,128)(2,1)} %pad_maximum_fusion.7), channel_id=1, source_target_pairs={{4,12},{12,20},{20,28},{8,0},{16,8},{24,16},{5,13},{13,21},{21,29}... | collective-permute-start | bytes 1572872 | tf_op jit(solution)/shard_map/ppermute | solution.py:239
  80.0 33.1 %collective-permute-start.13 = (bf16[2,512,256]{2,1,0:T(8,128)(2,1)}, bf16[2,512,256]{2,1,0:T(8,128)(2,1)}, u32[]{:S(2)}, u32[]{:S(2)}) collective-permute-start(bf16[2,512,256]{2,1,0:T(8,128)(2,1)} %copy-done.14), channel_id=1, source_target_pairs={{0,2},{2,0},{1,3},{3,1},{4,6},{6,4},{5,7},{7,5},{8,10},{10,8},{9,1... | collective-permute-start | bytes 1572872 | tf_op jit(solution)/shard_map/ppermute | solution.py:242
  92.3 21.4 %collective-permute-start.14 = (bf16[2,512,256]{2,1,0:T(8,128)(2,1)}, bf16[2,512,256]{2,1,0:T(8,128)(2,1)}, u32[]{:S(2)}, u32[]{:S(2)}) collective-permute-start(bf16[2,512,256]{2,1,0:T(8,128)(2,1)} %copy-done.14), channel_id=1, source_target_pairs={{0,8},{8,16},{16,24},{12,4},{20,12},{28,20},{1,9},{9,17},{17,25},{... | collective-permute-start | bytes 1572872 | tf_op jit(solution)/shard_map/ppermute | solution.py:240
  111.8 22.5 %collective-permute-start.2 = (bf16[2,512,256]{2,1,0:T(8,128)(2,1)}, bf16[2,512,256]{2,1,0:T(8,128)(2,1)}, u32[]{:S(2)}, u32[]{:S(2)}) collective-permute-start(bf16[2,512,256]{2,1,0:T(8,128)(2,1)} %pad_maximum_fusion.6), channel_id=1, source_target_pairs={{0,2},{2,0},{1,3},{3,1},{4,6},{6,4},{5,7},{7,5},{8,10},{10,8},{9,1... | collective-permute-start | bytes 1572872 | tf_op jit(solution)/shard_map/ppermute | solution.py:241
  111.8 23.4 %collective-permute-start.5 = (bf16[2,512,256]{2,1,0:T(8,128)(2,1)}, bf16[2,512,256]{2,1,0:T(8,128)(2,1)}, u32[]{:S(2)}, u32[]{:S(2)}) collective-permute-start(bf16[2,512,256]{2,1,0:T(8,128)(2,1)} %pad_maximum_fusion.6), channel_id=1, source_target_pairs={{4,12},{12,20},{20,28},{8,0},{16,8},{24,16},{5,13},{13,21},{21,29}... | collective-permute-start | bytes 1572872 | tf_op jit(solution)/shard_map/ppermute | solution.py:239
  113.2 23.3 %collective-permute-start.3 = (bf16[2,512,256]{2,1,0:T(8,128)(2,1)}, bf16[2,512,256]{2,1,0:T(8,128)(2,1)}, u32[]{:S(2)}, u32[]{:S(2)}) collective-permute-start(bf16[2,512,256]{2,1,0:T(8,128)(2,1)} %collective-permute-done), channel_id=1, source_target_pairs={{0,2},{2,0},{1,3},{3,1},{4,6},{6,4},{5,7},{7,5},{8,10},{10,8},{9,1... | collective-permute-start | bytes 1572872 | tf_op jit(solution)/shard_map/ppermute | solution.py:242
  113.7 22.7 %collective-permute-start.4 = (bf16[2,512,256]{2,1,0:T(8,128)(2,1)}, bf16[2,512,256]{2,1,0:T(8,128)(2,1)}, u32[]{:S(2)}, u32[]{:S(2)}) collective-permute-start(bf16[2,512,256]{2,1,0:T(8,128)(2,1)} %collective-permute-done), channel_id=1, source_target_pairs={{0,8},{8,16},{16,24},{12,4},{20,12},{28,20},{1,9},{9,17},{17,25},{... | collective-permute-start | bytes 1572872 | tf_op jit(solution)/shard_map/ppermute | solution.py:240
  121.3 43.1 %collective-permute-start.9 = (bf16[768,1536]{1,0:T(8,128)(2,1)}, bf16[768,1536]{1,0:T(8,128)(2,1)}, u32[]{:S(2)}, u32[]{:S(2)}) collective-permute-start(bf16[768,1536]{1,0:T(8,128)(2,1)} %collective-permute-done.8), channel_id=1, source_target_pairs={{0,2},{2,0},{1,3},{3,1},{4,6},{6,4},{5,7},{7,5},{8,10},{10,8},{9,1... | collective-permute-start | bytes 7077896 | tf_op jit(solution)/shard_map/ppermute | solution.py:217
  134.4 23.4 %collective-permute-start.24 = (bf16[512,256]{1,0:T(8,128)(2,1)}, bf16[512,256]{1,0:T(8,128)(2,1)}, u32[]{:S(2)}, u32[]{:S(2)}) collective-permute-start(bf16[512,256]{1,0:T(8,128)(2,1)} %get-tuple-element.42), channel_id=1, source_target_pairs={{0,4},{4,0},{8,12},{12,8},{16,20},{20,16},{24,28},{28,24},{1,5},{5... | collective-permute-start | bytes 786440 | tf_op jit(solution)/shard_map/ppermute | solution.py:252
  135.3 25.0 %collective-permute-start.16 = (bf16[512,256]{1,0:T(8,128)(2,1)}, bf16[512,256]{1,0:T(8,128)(2,1)}, u32[]{:S(2)}, u32[]{:S(2)}) collective-permute-start(bf16[512,256]{1,0:T(8,128)(2,1)} %get-tuple-element.40), channel_id=1, source_target_pairs={{0,4},{4,0},{8,12},{12,8},{16,20},{20,16},{24,28},{28,24},{1,5},{5... | collective-permute-start | bytes 786440 | tf_op jit(solution)/shard_map/ppermute | solution.py:252
  161.3 23.7 %collective-permute-start.17 = (bf16[512,512]{1,0:T(8,128)(2,1)S(1)}, bf16[512,512]{1,0:T(8,128)(2,1)S(1)}, u32[]{:S(2)}, u32[]{:S(2)}) collective-permute-start(bf16[512,512]{1,0:T(8,128)(2,1)S(1)} %pad_maximum_fusion.12), channel_id=1, source_target_pairs={{0,1},{1,0},{2,3},{3,2},{4,5},{5,4},{6,7},{7,6},{8,9},{9,8},{10,11... | collective-permute-start | bytes 1572872 | tf_op jit(solution)/shard_map/ppermute | solution.py:254
  163.1 31.0 %collective-permute-start.7 = (bf16[512,512]{1,0:T(8,128)(2,1)S(1)}, bf16[512,512]{1,0:T(8,128)(2,1)S(1)}, u32[]{:S(2)}, u32[]{:S(2)}) collective-permute-start(bf16[512,512]{1,0:T(8,128)(2,1)S(1)} %pad_maximum_fusion.10), channel_id=1, source_target_pairs={{0,1},{1,0},{2,3},{3,2},{4,5},{5,4},{6,7},{7,6},{8,9},{9,8},{10,11... | collective-permute-start | bytes 1572872 | tf_op jit(solution)/shard_map/ppermute | solution.py:254
  (23 other events, 150.0 us)
Sparse Core Ops, SparseCore 0:
  25.5 29.4 all-gather.10
  56.6 34.8 all-gather.8
  93.0 35.4 all-gather.6

commit v2 on v0

--- a/solution.py
+++ b/solution.py
@@ -1,12 +1,19 @@
+import functools
 import math
 
 import jax
 import jax.numpy as jnp
 from jax import lax
+from jax.experimental import pallas as pl
+from jax.experimental.pallas import tpu as pltpu
 from jax.sharding import PartitionSpec as P
 
 HD = 128
 BLOCK = 128
+Q_ROWS = 256
+AHEAD = 2
+MESH = pl.DeviceIdType.MESH
+EXP2_SCALE = math.log2(math.e) / math.sqrt(HD)
 
 
 def with_halo(array, sides, width):
@@ -22,7 +29,7 @@
     return array
 
 
-def local(queries, keys, values, residual, gate, out_weight, far_list, far_count):
+def plain_local(queries, keys, values, residual, gate, out_weight, far_list, far_count):
     tile_rows, width_here = queries.shape
     heads_here = width_here // HD
     scale = 1.0 / math.sqrt(HD)
@@ -104,7 +111,358 @@
     return (residual.astype(jnp.float32) + gate[None, :] * summed).astype(jnp.bfloat16)
 
 
+def attend_rows(q, pieces):
+    f32 = jnp.float32
+    scores = []
+    for k, _, bias in pieces:
+        s = lax.dot_general(q, k, (((1,), (1,)), ((), ())), preferred_element_type=f32)
+        scores.append(s if bias is None else s + bias)
+    largest = scores[0].max(axis=1, keepdims=True)
+    for s in scores[1:]:
+        largest = jnp.maximum(largest, s.max(axis=1, keepdims=True))
+    total = jnp.zeros((q.shape[0], 2 * HD), f32)
+    for s, (_, v, _) in zip(scores, pieces):
+        weights = jnp.exp2((s - largest) * EXP2_SCALE).astype(jnp.bfloat16)
+        v_ones = jnp.concatenate([v, jnp.ones_like(v)], axis=1)
+        total = total + jnp.dot(weights, v_ones, preferred_element_type=f32)
+    return (total[:, :HD] / total[:, HD:]).astype(jnp.bfloat16)
+
+
+def paired_kernel(
+    n_z, pick, near_bias, far_bias, keys, values, queries, weight, att, w_other,
+    got, near_mine, near_got, side_mine, side_got, far, done,
+    x_send, x_recv, direct_send, direct_recv, onward_send, onward_recv,
+    side_send, side_recv, pass_send, pass_recv, up_send, down_send, far_recv,
+    back_send, back_recv, y_send, y_recv, w_send, w_recv,
+):
+    frame, row, group_y = lax.axis_index("tm"), lax.axis_index("height"), lax.axis_index("heads")
+    x, z = frame % 2, frame // 2
+    rows, width = keys.shape
+    half = width // 2
+    n_heads = half // HD
+    per_tile = rows // BLOCK
+    above, below = z < n_z - 1, z > 0
+    partner = frame + 1 - 2 * x
+    direct_to = jnp.where(x == 1, frame + 2, frame - 2)
+    onward_to = jnp.where(x == 1, frame - 2, frame + 2)
+    direct_out = (x == 1) & above | (x == 0) & below
+    direct_in = (x == 1) & below | (x == 0) & above
+
+    def cols(start, h):
+        return pl.ds(pl.multiple_of(start + h * HD, HD), HD)
+
+    def mine_cols(h):
+        return cols(x * half, h)
+
+    def remote(src, dst, send, recv, to):
+        return pltpu.make_async_remote_copy(
+            src_ref=src, dst_ref=dst, send_sem=send, recv_sem=recv,
+            device_id=to, device_id_type=MESH,
+        )
+
+    def x_copy(h, a):
+        src = (keys, values, queries)[a].at[:, cols((1 - x) * half, h)]
+        return remote(src, got.at[h, a], x_send.at[h, a], x_recv.at[h, a], {"tm": partner})
+
+    def direct_copy(h, a):
+        src = (keys, values)[a].at[:, mine_cols(h)]
+        return remote(src, near_got.at[h, a], direct_send.at[h, a], direct_recv.at[h, a], {"tm": direct_to})
+
+    def side_copy(h, a):
+        src = (keys, values)[a].at[:, mine_cols(h)]
+        return remote(src, side_mine.at[h, a], side_send.at[h, a], side_recv.at[h, a], {"height": 1 - row})
+
+    def onward_copy(h):
+        return remote(got.at[h, pl.ds(0, 2)], near_mine.at[h], onward_send.at[h], onward_recv.at[h], {"tm": onward_to})
+
+    def pass_copy(h):
+        return remote(got.at[h, pl.ds(0, 2)], side_got.at[h], pass_send.at[h], pass_recv.at[h], {"height": 1 - row})
+
+    def up_copy(h, o):
+        return remote(far.at[h, o], far.at[h, o], up_send.at[h, o], far_recv.at[h, o], {"tm": frame + 2})
+
+    def down_copy(h, o):
+        return remote(far.at[h, o], far.at[h, o], down_send.at[h, o], far_recv.at[h, o], {"tm": frame - 2})
+
+    def back_copy(h):
+        return remote(done.at[h], att.at[:, mine_cols(h)], back_send.at[h], back_recv.at[h], {"tm": partner})
+
+    def y_copy(h, a):
+        start = x * half if a == 0 else (1 - x) * half
+        src = att.at[:, cols(start, h)]
+        dst = att.at[:, cols(width + start, h)]
+        return remote(src, dst, y_send.at[h, a], y_recv.at[h, a], {"heads": 1 - group_y})
+
+    wide = width // 2
+
+    def w_copy():
+        src = weight.at[pl.ds(row * wide, wide), pl.ds(pl.multiple_of((1 - group_y) * width, width), width)]
+        return remote(src, w_other.at[pl.ds(row * wide, wide)], w_send.at[0], w_recv.at[0], {"heads": 1 - group_y})
+
+    def w_pass():
+        part = w_other.at[pl.ds(row * wide, wide)]
+        return remote(part, part, w_send.at[1], w_recv.at[1], {"height": 1 - row})
+
+    barrier = pltpu.get_barrier_semaphore()
+    for to in ({"tm": partner}, {"height": 1 - row}, {"heads": 1 - group_y}):
+        pl.semaphore_signal(barrier, inc=1, device_id=to, device_id_type=MESH)
+
+    @pl.when(above)
+    def _():
+        pl.semaphore_signal(barrier, inc=1, device_id={"tm": frame + 2}, device_id_type=MESH)
+
+    @pl.when(below)
+    def _():
+        pl.semaphore_signal(barrier, inc=1, device_id={"tm": frame - 2}, device_id_type=MESH)
+
+    pl.semaphore_wait(barrier, 3 + above.astype(jnp.int32) + below.astype(jnp.int32))
+
+    def start_head(h):
+        for a in range(2):
+            x_copy(h, a).start()
+            side_copy(h, a).start()
+
+        @pl.when(direct_out)
+        def _():
+            for a in range(2):
+                direct_copy(h, a).start()
+
+        x_copy(h, 2).start()
+
+    lax.fori_loop(0, AHEAD, lambda h, c: (start_head(h), c)[1], 0)
+    w_copy().start()
+
+    @pl.when(jnp.logical_not(direct_in))
+    def _():
+        near_got[...] = jnp.zeros_like(near_got)
+
+    @pl.when(jnp.logical_not(direct_out))
+    def _():
+        near_mine[...] = jnp.zeros_like(near_mine)
+
+    def offered(block, p):
+        total = jnp.zeros((BLOCK, HD), jnp.float32)
+        for b in range(per_tile):
+            total = total + block(b).astype(jnp.float32) * pick[p, b]
+        return total.astype(jnp.bfloat16)
+
+    def arrive(h):
+        for a in range(2):
+            x_copy(h, a).wait_recv()
+
+        @pl.when(direct_in)
+        def _():
+            onward_copy(h).start()
+
+        pass_copy(h).start()
+        for a, own in enumerate((keys, values)):
+            far[h, z, 0, a] = offered(lambda b: own[b * BLOCK : (b + 1) * BLOCK, mine_cols(h)], 0)
+            far[h, z, 1, a] = offered(lambda b: got[h, a, b * BLOCK : (b + 1) * BLOCK], 1)
+
+        @pl.when(above)
+        def _():
+            up_copy(h, z).start()
+
+        @pl.when(below)
+        def _():
+            down_copy(h, z).start()
+
+    def hop(h, k):
+        @pl.when(z >= k)
+        def _():
+            up_copy(h, z - k).wait_recv()
+
+            @pl.when(above)
+            def _():
+                up_copy(h, z - k).start()
+
+        @pl.when(z + k < n_z)
+        def _():
+            down_copy(h, z + k).wait_recv()
+
+            @pl.when(below)
+            def _():
+                down_copy(h, z + k).start()
+
+    def compute(h):
+        x_copy(h, 2).wait_recv()
+        for a in range(2):
+            side_copy(h, a).wait_recv()
+        pass_copy(h).wait_recv()
+
+        @pl.when(direct_in)
+        def _():
+            for a in range(2):
+                direct_copy(h, a).wait_recv()
+
+        @pl.when(direct_out)
+        def _():
+            onward_copy(h).wait_recv()
+
+        k_mine, v_mine = keys[:, mine_cols(h)], values[:, mine_cols(h)]
+        far_k = far[h, :, :, 0].reshape(n_z * 2 * BLOCK, HD)
+        far_v = far[h, :, :, 1].reshape(n_z * 2 * BLOCK, HD)
+        pair = [(k_mine, v_mine, None), (got[h, 0], got[h, 1], None)]
+        theirs = pair + [
+            (side_got[h, 0], side_got[h, 1], None),
+            (near_got[h, 0], near_got[h, 1], near_bias[1:2]),
+            (far_k, far_v, far_bias[1:2]),
+        ]
+        for q0 in range(0, rows, Q_ROWS):
+            done[h, q0 : q0 + Q_ROWS] = attend_rows(got[h, 2, q0 : q0 + Q_ROWS], theirs)
+        back_copy(h).start()
+        ours = pair + [
+            (side_mine[h, 0], side_mine[h, 1], None),
+            (near_mine[h, 0], near_mine[h, 1], near_bias[0:1]),
+            (far_k, far_v, far_bias[0:1]),
+        ]
+        for q0 in range(0, rows, Q_ROWS):
+            att[q0 : q0 + Q_ROWS, mine_cols(h)] = attend_rows(
+                queries[q0 : q0 + Q_ROWS, mine_cols(h)], ours
+            )
+        y_copy(h, 0).start()
+
+    def across(h):
+        remote(
+            done.at[h], att.at[:, cols((1 - x) * half, h)], back_send.at[h], back_recv.at[h], {"tm": partner}
+        ).wait_recv()
+        y_copy(h, 1).start()
+
+    def stage(i, lag, work):
+        @pl.when((i >= lag) & (i - lag < n_heads))
+        def _():
+            work(i - lag)
+
+    def step(i, carry):
+        @pl.when(i + AHEAD < n_heads)
+        def _():
+            start_head(i + AHEAD)
+
+        stage(i, 0, arrive)
+        for k in range(1, n_z):
+            stage(i, k, lambda h, k=k: hop(h, k))
+        stage(i, n_z - 1, compute)
+        stage(i, n_z, across)
+
+        @pl.when(i == n_heads)
+        def _():
+            w_copy().wait_recv()
+            w_pass().start()
+
+        return carry
+
+    lax.fori_loop(0, n_heads + n_z, step, 0)
+
+    def finish(h, carry):
+        for a in range(3):
+            x_copy(h, a).wait_send()
+        for a in range(2):
+            side_copy(h, a).wait_send()
+            y_copy(h, a).wait_send()
+            y_copy(h, a).wait_recv()
+        pass_copy(h).wait_send()
+        back_copy(h).wait_send()
+
+        @pl.when(direct_out)
+        def _():
+            for a in range(2):
+                direct_copy(h, a).wait_send()
+
+        @pl.when(direct_in)
+        def _():
+            onward_copy(h).wait_send()
+
+        for o in range(n_z):
+            @pl.when(above & (z >= o))
+            def _():
+                up_copy(h, o).wait_send()
+
+            @pl.when(below & (z <= o))
+            def _():
+                down_copy(h, o).wait_send()
+
+        return carry
+
+    lax.fori_loop(0, n_heads, finish, 0)
+    w_copy().wait_send()
+    w_pass().wait_send()
+    other = w_other.at[pl.ds((1 - row) * wide, wide)]
+    remote(other, other, w_send.at[1], w_recv.at[1], {"height": 1 - row}).wait_recv()
+
+
+def paired_local(queries, keys, values, residual, gate, out_weight, far_list, far_count):
+    rows, width = queries.shape
+    n_frames, n_rows = lax.axis_size("tm"), lax.axis_size("height")
+    frame, row = lax.axis_index("tm"), lax.axis_index("height")
+    group_y = lax.axis_index("heads")
+    x, z = frame % 2, frame // 2
+    n_z = n_frames // 2
+    n_heads = width // 2 // HD
+    per_tile = rows // BLOCK
+    far_entries = far_list.shape[1]
+    f32 = jnp.float32
+
+    listed_ok = jnp.arange(far_entries)[None, :] < far_count[:, None]
+    own_tiles = jnp.stack([frame, frame ^ 1]) * n_rows + row
+    named = listed_ok[None] & (far_list[None] // per_tile == own_tiles[:, None, None])
+    offered = jnp.max(jnp.where(named, far_list[None] % per_tile, 0), axis=(1, 2))
+    pick = (offered[:, None] == jnp.arange(per_tile)[None, :]).astype(f32)
+    source = far_list[own_tiles] // per_tile // n_rows
+    slot_frames = jnp.arange(n_frames) ^ x
+    live = (source[:, :, None] == slot_frames[None, None, :]) & listed_ok[own_tiles][:, :, None]
+    far_bias = jnp.repeat(jnp.where(jnp.any(live, axis=1), f32(0), f32(-1e30)), BLOCK, axis=1)
+    near_ok = jnp.where(jnp.stack([x, x ^ 1]) == 0, z > 0, z < n_z - 1)
+    near_bias = jnp.broadcast_to(jnp.where(near_ok, f32(0), f32(-1e30))[:, None], (2, rows))
+
+    bf16 = jnp.bfloat16
+    vmem, dma = pltpu.VMEM, pltpu.SemaphoreType.DMA
+    any_spec, vmem_spec = pl.BlockSpec(memory_space=pl.ANY), pl.BlockSpec(memory_space=pltpu.VMEM)
+    pair_buffer = vmem((n_heads, 2, rows, HD), bf16)
+    keys_seen = 4 * rows + n_frames * BLOCK
+    att, w_other = pl.pallas_call(
+        functools.partial(paired_kernel, n_z),
+        out_shape=[
+            jax.ShapeDtypeStruct((rows, 2 * width), bf16),
+            jax.ShapeDtypeStruct((width, width), bf16),
+        ],
+        in_specs=[pl.BlockSpec(memory_space=pltpu.SMEM)] + [vmem_spec] * 5 + [any_spec],
+        out_specs=[vmem_spec, any_spec],
+        scratch_shapes=[vmem((n_heads, 3, rows, HD), bf16)]
+        + [pair_buffer] * 4
+        + [vmem((n_heads, n_z, 2, 2, BLOCK, HD), bf16), vmem((n_heads, rows, HD), bf16)]
+        + [dma((n_heads, 3))] * 2
+        + [dma((n_heads, 2))] * 2
+        + [dma((n_heads,))] * 2
+        + [dma((n_heads, 2))] * 2
+        + [dma((n_heads,))] * 2
+        + [dma((n_heads, n_z))] * 3
+        + [dma((n_heads,))] * 2
+        + [dma((n_heads, 2))] * 2
+        + [dma((2,))] * 2,
+        compiler_params=pltpu.CompilerParams(
+            collective_id=0, has_side_effects=True, vmem_limit_bytes=56 * 2**20
+        ),
+        cost_estimate=pl.CostEstimate(
+            flops=8 * rows * keys_seen * width, bytes_accessed=30 * rows * width,
+            transcendentals=rows * keys_seen * width // HD,
+        ),
+    )(pick, near_bias, far_bias, keys, values, queries, out_weight)
+    w_own = lax.dynamic_slice(out_weight, (0, group_y * width), (width, width))
+    projected = jnp.dot(att[:, :width], w_own, preferred_element_type=f32)
+    projected = projected + jnp.dot(att[:, width:], w_other, preferred_element_type=f32)
+    return (residual.astype(f32) + gate[None, :] * projected).astype(bf16)
+
+
 def solution(mesh):
+    sizes = dict(mesh.shape)
+
+    def local(queries, *rest):
+        width = queries.shape[1]
+        paired = sizes["tm"] % 2 == 0 and sizes["height"] == 2 and sizes["heads"] == 2
+        if paired and width % (2 * HD) == 0:
+            return paired_local(queries, *rest)
+        return plain_local(queries, *rest)
+
     return jax.shard_map(
         local,
         mesh=mesh,

time: 461 us -> 136 us (0.30)
  waiting for transfers between devices: 219 us -> 0 us
  Pallas kernels: 0 us -> 119 us
  matrix products: 100 us -> 8.9 us
  other arithmetic: 70.4 us -> 2.63 us
  local copies, waits for them, and re-layouts: 35.5 us -> 5.09 us
  starting transfers between devices: 18.5 us -> 0 us
  between operations: 14.1 us -> 0.06 us
    ppermute x4 -> x0, waiting for transfers between devices: 173 us -> none  [the longest x2 173 us: with_halo(): before = lax.ppermute(last, axis, up)]
    pallas_call x0 -> x1, Pallas kernels: none -> 119 us  [paired_local(): pl.pallas_call(functools.partial(paired_kernel, n_z), out_shape=[jax.Shap...]
    dot_general x7 -> x2, matrix products: 100 us -> 8.9 us  [the longest x1 5.08 us: paired_local(): jnp.dot(att[:, width:], w_other, preferred_element_type=f32)]
    reduce_scatter x1 -> x0, waiting for transfers between devices: 45.7 us -> none  [local(): lax.psum_scatter(projected.astype(jnp.bfloat16), 'heads', scatter_dimensi...]
    reduce_sum x3 -> x0, other arithmetic: 36.8 us -> none  [the longest x2 36.7 us: attend(): total = total * fade + jnp.sum(weights, axis=-1)]
    concatenate x2 -> x0, other arithmetic: 20.3 us -> none  [the longest x1 16.1 us: local(): first_kv = jnp.concatenate([key_vals, prior_tile, next_tile], axis=0)]
    slice x2 -> x0, local copies, waits for them, and re-layouts: 13.9 us -> none  [the longest x1 7.94 us: attend(): value_heads = block_kv[:, width_here:].reshape(-1, heads_here, HD)]
    ppermute x4 -> x0, starting transfers between devices: 11 us -> none  [the longest x2 8.48 us: with_halo(): before = lax.ppermute(last, axis, up)]
  transfers between devices with their start and end apart: 6 -> 0, of which waited for: 2 -> 0; matrix products, arithmetic and copies ran while one was open for 13% -> 0% of each run, Pallas kernels for 0% -> 0%
where the time goes in v2:
time: 136 us
  Pallas kernels  119 us (88%)
  matrix products  8.9 us (7%)
  local copies, waits for them, and re-layouts  5.09 us (4%)
  other arithmetic  2.63 us (2%)
    pallas_call x1, Pallas kernels, paired_local(): pl.pallas_call(functools.partial(paired_kernel, n_z), out_shape=[jax.Shap...  119 us
    dot_general x1, matrix products, paired_local(): jnp.dot(att[:, width:], w_other, preferred_element_type=f32)  5.08 us
    dot_general x1, matrix products, paired_local(): projected = jnp.dot(att[:, :width], w_own, preferred_element_type=f32)  3.82 us
    unnamed x11, local copies, waits for them, and re-layouts  3.23 us

profile of v2, /device:TPU:0, one launch (start us, length us, event | category | flops | bytes accessed | tf_op | source)
XLA Modules:
  0.0 135.6 jit_solution(10348458197631540767)
XLA Ops:
  0.0 0.1 select_select_fusion
  0.1 0.1 fusion.19
  0.2 0.1 fusion.18
  0.2 0.7 iota_compare_fusion
  1.0 0.1 copy.12
  1.1 0.6 gather_fusion.1
  1.6 0.7 broadcast_in_dim.65.near_bias
  2.3 0.7 add_select_fusion.1
  3.0 0.2 select_reduce_fusion
  3.2 0.7 compare_convert_fusion.pick
  3.8 0.8 copy.13
  4.6 0.6 gather_fusion
  5.2 0.1 and_reduce_fusion
  5.3 0.1 broadcast_bitcast_fusion
  5.3 0.6 copy.16
  5.9 118.9 %shard_map.82 = (bf16[512,3072]{1,0:T(8,128)(2,1)}, bf16[1536,1536]{1,0:T(8,128)(2,1)}) custom-call(f32[2,4]{1,0:T(2,128)} %compare_convert_fusion.pick, f32[2,512]{1,0:T(2,128)} %broadcast_in_dim.65.near_bias, f32[2,1024]{1,0:T(2,128)} %bitcast.14, bf16[512,1536]{1,0:T(8,128)(2,1)} %keys.1, bf16[512,1536]{1,0:T(8,128)(2,1)} %values.1, ...), custom_call_target="tpu_custom_call" | custom-call | flops 19327352832 | bytes 23592960 | tf_op jit(solution)/shard_map/pallas_call | solution.py:422
  124.9 0.0 copy-start
  124.9 0.0 copy-start.1
  124.9 0.0 copy-start.2
  124.9 5.1 %fusion.14 = f32[512,1536]{1,0:T(8,128)S(1)} fusion(bf16[1536,1536]{1,0:T(8,128)(2,1)} %get-tuple-element.8, bf16[512,3072]{1,0:T(8,128)(2,1)} %get-tuple-element.7), kind=kOutput, calls=%fused_computation.8 | convolution fusion | flops 2415919104 | bytes 9437184 | tf_op jit(solution)/shard_map/dot_general | solution.py:452
  130.0 0.4 copy-done
  130.4 0.4 copy-done.1
  130.8 0.9 copy-done.3
  131.8 3.8 %fusion.11 = bf16[512,1536]{1,0:T(8,128)(2,1)} fusion(f32[512,1536]{1,0:T(8,128)S(1)} %fusion.14, bf16[1536,3072]{1,0:T(8,128)(2,1)S(1)} %copy-done, s32[]{:T(128)S(6)} %select_n.89, bf16[512,1536]{1,0:T(8,128)(2,1)S(1)} %copy-done.1, bf16[512,3072]{1,0:T(8,128)(2,1)S(1)} %copy-done.3, f32[1536]{0:T(1024)S(1)} %copy-done.2), kind=kOutput, calls=%fused_computation.7 | convolution fusion | flops 2419851264 | bytes 12591108 | tf_op jit(solution)/shard_map/dot_general | solution.py:451
  (6 shorter events, 0.0 us)
Async XLA Ops:
  124.9 5.5 %copy-start = (bf16[1536,3072]{1,0:T(8,128)(2,1)S(1)}, bf16[1536,3072]{1,0:T(8,128)(2,1)}, u32[]{:S(2)}) copy-start(bf16[1536,3072]{1,0:T(8,128)(2,1)} %weight.1) | copy-start | bytes 28311556
  124.9 5.9 %copy-start.1 = (bf16[512,1536]{1,0:T(8,128)(2,1)S(1)}, bf16[512,1536]{1,0:T(8,128)(2,1)}, u32[]{:S(2)}) copy-start(bf16[512,1536]{1,0:T(8,128)(2,1)} %param.11) | copy-start | bytes 4718596
  124.9 5.9 %copy-start.2 = (f32[1536]{0:T(1024)S(1)}, f32[1536]{0:T(1024)}, u32[]{:S(2)}) copy-start(f32[1536]{0:T(1024)} %param.12) | copy-start | bytes 18436
  124.9 6.9 %copy-start.3 = (bf16[512,3072]{1,0:T(8,128)(2,1)S(1)}, bf16[512,3072]{1,0:T(8,128)(2,1)}, u32[]{:S(2)}) copy-start(bf16[512,3072]{1,0:T(8,128)(2,1)} %get-tuple-element.7) | copy-start | bytes 9437188
